TPU v7x, 512 devices: a whole 4x8x8 slice. The times are simulated.
512 devices in a mesh: tm: 64 (over z_hi, y, x), head: 8 (over z_lo, core).
Axes of the slice: x: 4, y: 8, z: 8 (z_hi: 2, z_lo: 4; z = z_hi * 4 + z_lo), core: 2. Of those that a mesh axis runs over, the one named last changes fastest.
Arguments:
- frames_in: bfloat16 [64, 1024, 1024], P('tm', 'head'), may hold values from -400 to 400
- in_weight: bfloat16 [1024, 5120], P('tm', 'head'), may hold values from -0.1875 to 0.1875
- out_weight: bfloat16 [1024, 1024], replicated, may hold values from -0.1875 to 0.1875
- block_ids: int32 [1024], replicated, may hold values from 0 to 15, as said below
- block_lists: int32 [16, 4], replicated, may hold values from 0 to 15, as said below
- decays: float32 [64, 16, 16], P('tm', 'head'), may hold values from 0.3 to 1
Outputs:
- layer_out: bfloat16 [64, 1024, 1024], P('tm', 'head')
Inputs may be any that keep to these rules, and one draw needn't show every extreme that they name: `block_ids`: each of the 16 block ids is held by exactly 64 tokens. `block_lists`: row g starts with g itself, followed by 4 - 1 further blocks, all different.
All inputs are finite; a program needn't handle non-finite values.
Results may differ from a plain program's by a relative error of at most 0.0069.
Values may be sent and summed in bfloat16 or wider, within the bound.
A program may use at most 128 MiB of HBM per device.

v0:
```python
import math
import jax
import jax.numpy as jnp
from jax import lax
from jax.sharding import PartitionSpec as P

HD = 64
N = 64
TOKS = 1024
NB = 16
epsilon = 1e-06


def carried_in(shard, axis, combine, identity):
    peers, index = (lax.axis_size(axis), lax.axis_index(axis))
    everything = jax.tree.map(lambda part: lax.all_gather(part, axis), shard)
    start = jax.tree.map(
        lambda part, zero: jnp.broadcast_to(jnp.asarray(zero, part.dtype), part.shape),
        shard,
        identity,
    )

    def step(k, before):
        reached = k < index
        new = combine(before, jax.tree.map(lambda part: part[k], everything))
        return jax.tree.map(lambda a, b: jnp.where(reached, a, b), new, before)

    return lax.fori_loop(0, peers, step, start)


def head_norm(values):
    wide = values.astype(jnp.float32)
    return (wide * lax.rsqrt(jnp.mean(wide * wide, axis=-1, keepdims=True) + epsilon)).astype(
        jnp.bfloat16
    )


def combine(earlier, after_it):
    return (earlier[0] * after_it[0], after_it[0][:, :, None] * earlier[1] + after_it[1])


def body(frames_in, in_weight, out_weight, block_ids, block_lists, decays):
    frame_count, local_tokens, feature_width = frames_in.shape
    heads_here = decays.shape[1]
    groups = decays.shape[2]
    tokens = block_ids.shape[0]
    block_size = tokens // groups
    head_size = HD
    state_size = N
    selected_count = block_lists.shape[1]
    inputs_wide = frames_in.astype(jnp.float32)
    normed = (
        inputs_wide
        * lax.rsqrt(jnp.mean(inputs_wide * inputs_wide, axis=-1, keepdims=True) + epsilon)
    ).astype(jnp.bfloat16)
    full_rows = lax.all_gather(in_weight, "tm", axis=0, tiled=True)
    flat_rows = normed.reshape(frame_count * local_tokens, feature_width)
    local_flat = jnp.dot(
        flat_rows,
        lax.all_gather(full_rows, "head", axis=1, tiled=True),
        preferred_element_type=jnp.float32,
    ).astype(jnp.bfloat16)
    local_proj = local_flat.reshape(frame_count, local_tokens, local_flat.shape[1])
    projected = lax.all_to_all(local_proj, "head", split_axis=2, concat_axis=1, tiled=True)
    projected = projected.reshape(frame_count, tokens, heads_here, 5, head_size)
    sort_order = jnp.argsort(block_ids, stable=True)
    inverse_order = jnp.argsort(sort_order, stable=True)
    sorted_proj = jnp.take(projected, sort_order, axis=1).reshape(
        frame_count, groups, block_size, heads_here, 5, head_size
    )
    queries = head_norm(sorted_proj[:, :, :, :, 0])
    key_rows = head_norm(sorted_proj[:, :, :, :, 1])
    values_sorted = sorted_proj[:, :, :, :, 2]
    map_sorted = sorted_proj[:, :, :, :, 3, :state_size]
    readers_sorted = sorted_proj[:, :, :, :, 4, :state_size].astype(jnp.float32)
    chosen_keys = jnp.take(key_rows, block_lists, axis=1).reshape(
        frame_count, groups, selected_count * block_size, heads_here, head_size
    )
    chosen_values = jnp.take(values_sorted, block_lists, axis=1).reshape(
        frame_count, groups, selected_count * block_size, heads_here, head_size
    )
    updates = jnp.einsum(
        "fgshn,fgshd->fhgnd", map_sorted, values_sorted, preferred_element_type=jnp.float32
    )
    local_state = jnp.zeros((heads_here, groups, state_size, head_size), jnp.float32)
    running = jnp.ones((heads_here, groups), jnp.float32)
    frame_at = 0
    local_state = decays[frame_at][:, :, None, None] * local_state + updates[frame_at]
    running = decays[frame_at] * running
    states = [local_state]
    products = [running]
    identity = (
        jnp.ones((heads_here, groups), jnp.float32),
        jnp.zeros((heads_here, groups, state_size * head_size), jnp.float32),
    )
    carried = carried_in(
        (running, local_state.reshape(heads_here, groups, state_size * head_size)),
        "tm",
        combine,
        identity,
    )
    incoming = carried[1].reshape(heads_here, groups, state_size, head_size)
    ssm_scale = 1.0 / (N * math.sqrt(TOKS // NB))
    frame_at = 0
    full_state = states[frame_at] + products[frame_at][:, :, None, None] * incoming
    readout_sorted = (
        jnp.einsum(
            "gshn,hgnd->gshd", readers_sorted[frame_at], full_state, precision=lax.Precision.HIGHEST
        )
        * ssm_scale
    )
    scores = jnp.einsum(
        "gshd,guhd->hgsu",
        queries[frame_at],
        chosen_keys[frame_at],
        preferred_element_type=jnp.float32,
    ) / math.sqrt(head_size)
    exponent = jnp.exp(scores)
    weights = (exponent / jnp.sum(exponent, axis=-1, keepdims=True)).astype(jnp.bfloat16)
    attended = jnp.einsum(
        "hgsu,guhd->gshd", weights, chosen_values[frame_at], preferred_element_type=jnp.float32
    )
    mixed_sorted = (
        (attended + readout_sorted).astype(jnp.bfloat16).reshape(tokens, heads_here * head_size)
    )
    frames_mixed = [jnp.take(mixed_sorted, inverse_order, axis=0)]
    mixed = jnp.stack(frames_mixed, axis=0)
    token_mix = lax.all_to_all(mixed, "head", split_axis=1, concat_axis=2, tiled=True)
    result = jnp.dot(
        token_mix.reshape(frame_count * local_tokens, token_mix.shape[2]),
        out_weight,
        preferred_element_type=jnp.float32,
    )
    return result.astype(jnp.bfloat16).reshape(frame_count, local_tokens, feature_width)


def solution(mesh):
    return jax.shard_map(
        body,
        mesh=mesh,
        in_specs=(P("tm", "head", None), P("tm", "head"), P(), P(), P(), P("tm", "head", None)),
        out_specs=P("tm", "head", None),
        check_vma=False,
    )
```

profile of v0, /device:TPU:1, one launch (start us, length us, event | category | flops | bytes accessed | tf_op | source)
XLA Modules:
  0.0 990.8 jit_solution(7445949897962662394)
XLA Ops:
  7.3 138.0 %all-gather.4.cloned.1.call-done = bf16[1024,640]{1,0:T(8,128)(2,1)} async-done(((bf16[16,640]{1,0:T(8,128)(2,1)}), bf16[1024,640]{1,0:T(8,128)(2,1)}) %all-gather.4.cloned.1.call-update) | async-done | bytes 1310736 | tf_op jit(solution)/shard_map/all_gather | solution.py:56
  146.4 112.3 %all-gather.6.cloned.1.call-done = bf16[1024,5120]{1,0:T(8,128)(2,1)} async-done(((bf16[1024,640]{1,0:T(8,128)(2,1)}), bf16[1024,5120]{1,0:T(8,128)(2,1)}) %all-gather.6.cloned.1.call-update) | async-done | bytes 10485776 | tf_op jit(solution)/shard_map/all_gather | solution.py:60
  258.7 5.7 fusion.1
  264.4 4.1 copy.51
  269.1 28.9 %reduce.4 = bf16[5120,128]{1,0:T(8,128)(2,1)S(1)} reduce(bf16[5120,1,128]{2,1,0:T(2,128)(2,1)} %bitcast.84, bf16[]{:T(256)} %broadcast.155), dimensions={1}, to_apply=%bitcast.66.reduce_sub_computation | reduce | bytes 2621442
  299.2 6.9 all-to-all-start
  306.1 4.4 sort.31
  310.6 26.9 %all-to-all-done = bf16[8,2,40960]{2,1,0:T(2,128)(2,1)S(1)} async-done(((bf16[8,2,40960]{2,1,0:T(2,128)(2,1)}), bf16[8,2,40960]{2,1,0:T(2,128)(2,1)S(1)}, u32[]{:S(2)}, u32[]{:S(2)}) %all-to-all-start) | async-done | bytes 1310752 | tf_op jit(solution)/shard_map/all_to_all | solution.py:64
  337.5 3.7 reshape.273
  341.2 1.9 copy.73
  345.4 6.2 copy.53
  351.6 13.9 %gather_fusion = bf16[1024,2,5,64]{3,1,2,0:T(2,128)(2,1)} fusion(bf16[1024,2,5,64]{3,1,2,0:T(2,128)(2,1)} %copy.53, s32[1024]{0:T(1024)S(1)} %fusion.28), kind=kCustom, calls=%fused_computation.2 | custom fusion | bytes 2625536 | tf_op jit(solution)/shard_map/jit(_take)/gather | solution.py:68
  365.4 2.1 copy.54
  370.9 1.9 broadcast_add_fusion
  373.2 4.4 sort.32
  377.6 194.0 %all_gather.14 = f32[64,2,16]{2,1,0:T(2,128)S(1)} all-gather(f32[1,2,16]{2,1,0:T(2,128)S(1)} %copy-done.4), channel_id=1, replica_groups=mesh['tm'=64,'head'=8] {'tm'}, dimensions={0}, use_global_device_ids=true | all-gather | bytes 8320 | tf_op jit(solution)/shard_map/all_gather | solution.py:16
  574.4 2.1 gather_fusion.3
  576.5 2.1 slice_bitcast_fusion
  578.5 2.2 gather_fusion.2
  580.7 4.7 broadcast_select_fusion.1
  585.4 4.3 copy.59
  589.7 4.3 squeeze_reshape.7
  594.0 4.3 copy.56
  598.3 4.3 squeeze_reshape.6
  604.1 2.1 fusion.2
  606.3 1.7 fusion.13
  608.0 273.5 %all-gather.8.cloned.1.call-done = f32[64,2,16,4096]{3,2,1,0:T(8,128)} async-done(((f32[1,2,16,4096]{3,2,1,0:T(8,128)}), f32[64,2,16,4096]{3,2,1,0:T(8,128)}) %all-gather.8.cloned.1.call-update) | async-done | bytes 33554448 | tf_op jit(solution)/shard_map/all_gather | solution.py:16
  881.5 77.4 %while.14 = (s32[]{:T(128)}, f32[2,16,4096]{2,1,0:T(8,128)S(1)}, s32[]{:T(128)}, f32[64,2,16]{2,1,0:T(2,128)S(1)}, f32[64,2,16,4096]{3,2,1,0:T(8,128)}, /*index=5*/s32[]{:T(128)}, s32[]{:T(128)}) while((s32[]{:T(128)}, f32[2,16,4096]{2,1,0:T(8,128)S(1)}, s32[]{:T(128)}, f32[64,2,16]{2,1,0:T(2,128)S(1)}, ...), condition=%wide.region_7.9_spmd.clone, body=%wide.region_6.8_spmd.clone.sunk | while | flops 524292 | bytes 1573353 | solution.py:28
  960.3 3.2 fusion.5
  964.2 3.2 gather_fusion.1
  968.0 2.3 reduce.5
  970.3 12.2 %all_to_all.30 = bf16[8,2,8192]{2,1,0:T(2,128)(2,1)S(1)} all-to-all(bf16[8,2,8192]{2,1,0:T(2,128)(2,1)S(1)} %reshape.274), channel_id=1, replica_groups=mesh['tm'=64,'head'=8] {'head'}, dimensions={0} | all-to-all | bytes 524288 | tf_op jit(solution)/shard_map/all_to_all | solution.py:128
  (187 shorter events, 93.8 us)
Async XLA Ops:
  6.5 976.5 %copy-start = (bf16[1024,1024]{1,0:T(8,128)(2,1)S(1)}, bf16[1024,1024]{1,0:T(8,128)(2,1)}, u32[]{:S(2)}) copy-start(bf16[1024,1024]{1,0:T(8,128)(2,1)} %param.12) | copy-start | bytes 6291460
  6.5 138.8 %all-gather.4.cloned.1.call-start = ((), (), s32[]{:S(2)}) async-start(), calls=%async_computation.2 | async-start | bytes 1331200 | tf_op jit(solution)/shard_map/all_gather | solution.py:56
  7.3 251.5 %all-gather.6.cloned.1.call-start = ((), (), s32[]{:S(2)}) async-start(), calls=%async_computation.3 | async-start | bytes 11796480 | tf_op jit(solution)/shard_map/all_gather | solution.py:60
  298.0 8.2 copy-start.6
  298.0 12.6 %copy-start.4 = (f32[1,2,16]{2,1,0:T(2,128)S(1)}, f32[1,2,16]{2,1,0:T(2,128)}, u32[]{:S(2)}) copy-start(f32[1,2,16]{2,1,0:T(2,128)} %param.15) | copy-start | bytes 388
  299.2 38.3 %all-to-all-start = ((bf16[8,2,40960]{2,1,0:T(2,128)(2,1)}), bf16[8,2,40960]{2,1,0:T(2,128)(2,1)S(1)}, u32[]{:S(2)}, u32[]{:S(2)}) async-start(bf16[8,2,40960]{2,1,0:T(2,128)(2,1)} %reshape.272), calls=%async_computation | async-start | bytes 2621440 | tf_op jit(solution)/shard_map/all_to_all | solution.py:64
  306.1 575.3 %all-gather.8.cloned.1.call-start = ((), (), s32[]{:S(2)}) async-start(), calls=%async_computation.4 | async-start | bytes 34078720 | tf_op jit(solution)/shard_map/all_gather | solution.py:16
  367.9 1.4 copy-start.1
  369.7 3.1 copy-start.2
  369.7 3.1 copy-start.5
  602.6 3.6 copy-start.3
Sparse Core Ops, SparseCore 0:
  11.9 133.4 all-gather.3
  147.4 111.2 all-gather.5
  373.0 508.4 all-gather.7
where the time goes:
time: 995 us; the launch traced here: 991 us
  waiting for transfers between devices  551 us (55%)
  blocking collectives  206 us (21%)
  other arithmetic  127 us (13%)
  local copies, waits for them, and re-layouts  69.2 us (7%)
  matrix products  14.2 us (1%)
  between operations  13.4 us (1%)
    all_gather x1, waiting for transfers between devices, carried_in(): everything = jax.tree.map(lambda part: lax.all_gather(part, axis), shard)  273 us
    all_gather x1, blocking collectives, carried_in(): everything = jax.tree.map(lambda part: lax.all_gather(part, axis), shard)  194 us
    all_gather x1, waiting for transfers between devices, body(): full_rows = lax.all_gather(in_weight, 'tm', axis=0, tiled=True)  138 us
    all_gather x1, waiting for transfers between devices, body(): lax.all_gather(full_rows, 'head', axis=1, tiled=True)  112 us
    select_n x64, other arithmetic, step(): return jax.tree.map(lambda a, b: jnp.where(reached, a, b), new, before)  74.9 us
    unnamed x3, other arithmetic  31.2 us
    all_to_all x1, waiting for transfers between devices, body(): lax.all_to_all(local_proj, 'head', split_axis=2, concat_axis=1, tiled=True)  26.9 us
  transfers between devices with their start and end apart: 4, of which 4 were waited for; matrix products, arithmetic and copies ran while one was open for 5% of the time, Pallas kernels for 0%

commit v1 on v0

--- a/solution.py
+++ b/solution.py
@@ -61,7 +61,12 @@
         preferred_element_type=jnp.float32,
     ).astype(jnp.bfloat16)
     local_proj = local_flat.reshape(frame_count, local_tokens, local_flat.shape[1])
-    projected = lax.all_to_all(local_proj, "head", split_axis=2, concat_axis=1, tiled=True)
+    projected = jnp.concatenate(
+        lax.all_to_all(
+            jnp.stack(jnp.split(local_proj, lax.axis_size("head"), axis=2)), "head", 0, 0
+        ),
+        axis=1,
+    )
     projected = projected.reshape(frame_count, tokens, heads_here, 5, head_size)
     sort_order = jnp.argsort(block_ids, stable=True)
     inverse_order = jnp.argsort(sort_order, stable=True)

time: 995 us -> 960 us (0.965)
  other arithmetic: 127 us -> 98.4 us
    unnamed x3 -> x2, other arithmetic: 31.2 us -> 2.21 us
    reshape x3 -> x0, local copies, waits for them, and re-layouts: 11.7 us -> none  [the longest x2 7.63 us: body(): projected = projected.reshape(frame_count, tokens, heads_here, 5, head_size)]
where the time goes in v1:
time: 960 us; the launch traced here: 956 us
  waiting for transfers between devices  551 us (57%)
  blocking collectives  206 us (21%)
  other arithmetic  98.4 us (10%)
  local copies, waits for them, and re-layouts  63.6 us (7%)
  matrix products  14.2 us (1%)
  between operations  13.4 us (1%)
    all_gather x1, waiting for transfers between devices, carried_in(): everything = jax.tree.map(lambda part: lax.all_gather(part, axis), shard)  273 us
    all_gather x1, blocking collectives, carried_in(): everything = jax.tree.map(lambda part: lax.all_gather(part, axis), shard)  194 us
    all_gather x1, waiting for transfers between devices, body(): full_rows = lax.all_gather(in_weight, 'tm', axis=0, tiled=True)  138 us
    all_gather x1, waiting for transfers between devices, body(): lax.all_gather(full_rows, 'head', axis=1, tiled=True)  112 us
    select_n x64, other arithmetic, step(): return jax.tree.map(lambda a, b: jnp.where(reached, a, b), new, before)  74.9 us
    all_to_all x1, waiting for transfers between devices, body(): lax.all_to_all(jnp.stack(jnp.split(local_proj, lax.axis_size('head'), axi...  26.9 us
  transfers between devices with their start and end apart: 4, of which 4 were waited for; matrix products, arithmetic and copies ran while one was open for 5% of the time, Pallas kernels for 0%

profile of v1, /device:TPU:1, one launch (start us, length us, event | category | flops | bytes accessed | tf_op | source)
XLA Modules:
  0.0 956.2 jit_solution(715328489524011374)
XLA Ops:
  7.3 138.0 %all-gather.4.cloned.1.call-done = bf16[1024,640]{1,0:T(8,128)(2,1)} async-done(((bf16[16,640]{1,0:T(8,128)(2,1)}), bf16[1024,640]{1,0:T(8,128)(2,1)}) %all-gather.4.cloned.1.call-update) | async-done | bytes 1310736 | tf_op jit(solution)/shard_map/all_gather | solution.py:56
  146.4 112.3 %all-gather.6.cloned.1.call-done = bf16[1024,5120]{1,0:T(8,128)(2,1)} async-done(((bf16[1024,640]{1,0:T(8,128)(2,1)}), bf16[1024,5120]{1,0:T(8,128)(2,1)}) %all-gather.6.cloned.1.call-update) | async-done | bytes 10485776 | tf_op jit(solution)/shard_map/all_gather | solution.py:60
  258.7 5.7 fusion.1
  269.8 6.9 all-to-all-start
  276.7 4.4 sort.31
  281.2 26.9 %all-to-all-done = bf16[8,1,128,640]{3,2,1,0:T(8,128)(2,1)S(1)} async-done(((bf16[8,1,128,640]{3,2,1,0:T(8,128)(2,1)}), bf16[8,1,128,640]{3,2,1,0:T(8,128)(2,1)S(1)}, u32[]{:S(2)}, u32[]{:S(2)}) %all-to-all-start) | async-done | bytes 1310752 | tf_op jit(solution)/shard_map/all_to_all | solution.py:65
  308.1 1.9 copy.66
  309.9 2.4 reshape.228
  312.3 4.2 copy.67
  316.5 13.9 %gather_fusion = bf16[1024,2,5,64]{3,1,2,0:T(2,128)(2,1)} fusion(bf16[1024,2,5,64]{3,1,2,0:T(2,128)(2,1)} %copy.67, s32[1024]{0:T(1024)S(1)} %fusion.36), kind=kCustom, calls=%fused_computation.2 | custom fusion | bytes 2625536 | tf_op jit(solution)/shard_map/jit(_take)/gather | solution.py:73
  330.3 2.1 copy.68
  332.8 1.4 copy-done.1
  335.8 1.9 broadcast_add_fusion
  337.8 4.4 sort.32
  342.5 194.3 %all_gather.14 = f32[64,2,16]{2,1,0:T(2,128)S(1)} all-gather(f32[1,2,16]{2,1,0:T(2,128)S(1)} %copy-done.4), channel_id=1, replica_groups=mesh['tm'=64,'head'=8] {'tm'}, dimensions={0}, use_global_device_ids=true | all-gather | bytes 8320 | tf_op jit(solution)/shard_map/all_gather | solution.py:16
  539.5 2.1 gather_fusion.3
  541.6 2.1 slice_bitcast_fusion
  543.7 2.2 gather_fusion.2
  545.9 4.7 broadcast_select_fusion.1
  550.6 4.3 copy.73
  554.9 4.3 squeeze_reshape.7
  559.2 4.3 copy.70
  563.5 4.3 squeeze_reshape.6
  567.8 1.5 fusion.9
  569.3 2.1 fusion.2
  571.4 1.7 fusion.13
  573.1 273.2 %all-gather.8.cloned.1.call-done = f32[64,2,16,4096]{3,2,1,0:T(8,128)} async-done(((f32[1,2,16,4096]{3,2,1,0:T(8,128)}), f32[64,2,16,4096]{3,2,1,0:T(8,128)}) %all-gather.8.cloned.1.call-update) | async-done | bytes 33554448 | tf_op jit(solution)/shard_map/all_gather | solution.py:16
  846.4 77.4 %while.14 = (s32[]{:T(128)}, f32[2,16,4096]{2,1,0:T(8,128)S(1)}, s32[]{:T(128)}, f32[64,2,16]{2,1,0:T(2,128)S(1)}, f32[64,2,16,4096]{3,2,1,0:T(8,128)}, /*index=5*/s32[]{:T(128)}, s32[]{:T(128)}) while((s32[]{:T(128)}, f32[2,16,4096]{2,1,0:T(8,128)S(1)}, s32[]{:T(128)}, f32[64,2,16]{2,1,0:T(2,128)S(1)}, ...), condition=%wide.region_7.9_spmd.clone, body=%wide.region_6.8_spmd.clone.sunk | while | flops 524292 | bytes 1573353 | solution.py:28
  925.2 3.2 fusion.5
  929.1 3.2 gather_fusion.1
  933.5 2.2 reduce.4
  935.8 12.2 %all_to_all.20 = bf16[8,2,8192]{2,1,0:T(2,128)(2,1)S(1)} all-to-all(bf16[8,2,8192]{2,1,0:T(2,128)(2,1)S(1)} %reshape.267), channel_id=1, replica_groups=mesh['tm'=64,'head'=8] {'head'}, dimensions={0} | all-to-all | bytes 524288 | tf_op jit(solution)/shard_map/all_to_all | solution.py:133
  (189 shorter events, 92.6 us)
Async XLA Ops:
  6.5 941.9 %copy-start = (bf16[1024,1024]{1,0:T(8,128)(2,1)S(1)}, bf16[1024,1024]{1,0:T(8,128)(2,1)}, u32[]{:S(2)}) copy-start(bf16[1024,1024]{1,0:T(8,128)(2,1)} %param.12) | copy-start | bytes 6291460
  6.5 138.8 %all-gather.4.cloned.1.call-start = ((), (), s32[]{:S(2)}) async-start(), calls=%async_computation.2 | async-start | bytes 1331200 | tf_op jit(solution)/shard_map/all_gather | solution.py:56
  7.3 251.5 %all-gather.6.cloned.1.call-start = ((), (), s32[]{:S(2)}) async-start(), calls=%async_computation.3 | async-start | bytes 11796480 | tf_op jit(solution)/shard_map/all_gather | solution.py:60
  266.4 10.3 %copy-start.6 = (s32[1024]{0:T(1024)S(1)}, s32[1024]{0:T(1024)}, u32[]{:S(2)}) copy-start(s32[1024]{0:T(1024)} %param.13) | copy-start | bytes 12292
  266.4 14.8 %copy-start.4 = (f32[1,2,16]{2,1,0:T(2,128)S(1)}, f32[1,2,16]{2,1,0:T(2,128)}, u32[]{:S(2)}) copy-start(f32[1,2,16]{2,1,0:T(2,128)} %param.15) | copy-start | bytes 388
  269.8 38.3 %all-to-all-start = ((bf16[8,1,128,640]{3,2,1,0:T(8,128)(2,1)}), bf16[8,1,128,640]{3,2,1,0:T(8,128)(2,1)S(1)}, u32[]{:S(2)}, u32[]{:S(2)}) async-start(bf16[8,1,128,640]{3,2,1,0:T(8,128)(2,1)} %fusion.27), calls=%async_computation | async-start | bytes 2621440 | tf_op jit(solution)/shard_map/all_to_all | solution.py:65
  276.7 569.7 %all-gather.8.cloned.1.call-start = ((), (), s32[]{:S(2)}) async-start(), calls=%async_computation.4 | async-start | bytes 34078720 | tf_op jit(solution)/shard_map/all_gather | solution.py:16
  332.8 1.4 copy-start.1
  334.6 3.1 copy-start.2
  334.6 7.5 copy-start.5
  567.8 3.6 copy-start.3
Sparse Core Ops, SparseCore 0:
  11.9 133.4 all-gather.3
  147.4 111.2 all-gather.5
  337.9 508.4 all-gather.7
